TPU v7x, 1024 devices: a whole 8x8x8 slice. The times are simulated.
1024 devices in a mesh: tm: 8 (over x), height: 16 (over z, core), expert: 8 (over y).
Axes of the slice: x: 8, y: 8, z: 8, core: 2. Of those that a mesh axis runs over, the one named last changes fastest.
Arguments:
- saved_conv: bfloat16 [32, 64, 16, 4096], P('tm', 'height', None, 'expert'), may hold values from -6 to 6
- grad_out: bfloat16 [32, 64, 16, 4096], P('tm', 'height', None, 'expert'), may hold values from -1.5 to 1.5
- conv_kernel: float32 [27, 4096], P(None, 'expert'), may hold values from -1 to 1
- weight_in: bfloat16 [8, 4096, 2048], P(None, 'expert', 'height'), may hold values from -0.09375 to 0.09375
- weight_out: bfloat16 [8, 2048, 4096], P(None, 'height', 'expert'), may hold values from -0.125 to 0.125
- gate_values: float32 [8, 8, 256], P('tm'), may hold values from 0.2 to 1
- picked_slots: int32 [8, 16, 8, 16], P('tm', 'height'), may hold values from 0 to 255, as said below
- slot_counts: int32 [8, 16, 8], P('tm', 'height'), may hold values from 0 to 16, as said below
Outputs:
- grad_input: float32 [32, 64, 16, 4096], P('tm', 'height', None, 'expert')
- grad_weight_in: float32 [8, 4096, 2048], P('tm', 'expert', 'height')
- grad_weight_out: float32 [8, 2048, 4096], P('tm', 'height', 'expert')
Inputs may be any that keep to these rules, and one draw needn't show every extreme that they name: `picked_slots`: the 16 indices of one expert for one frame block and row block are distinct; slots at or past the count are ignored. `slot_counts`: one expert has all 16 slots live for every frame block and row block.
All inputs are finite; a program needn't handle non-finite values.
Results may differ from a plain program's by a relative error of at most 0.015.
Values may be sent and summed in bfloat16 or wider, within the bound.
A program may use at most 64 MiB of HBM per device.

v0:
```python
import jax
import jax.numpy as jnp
from jax import lax
from jax.sharding import PartitionSpec as P


def extended(cells, sides, width):
    for axis, dim in sides:
        count = lax.axis_size(axis)
        ends = count - 1
        head = lax.slice_in_dim(cells, 0, width, axis=dim)
        tail = lax.slice_in_dim(cells, cells.shape[dim] - width, cells.shape[dim], axis=dim)
        cells = jnp.concatenate(
            [
                lax.ppermute(tail, axis, [(i, (i + 1) % count) for i in range(ends)]),
                cells,
                lax.ppermute(head, axis, [((i + 1) % count, i) for i in range(ends)]),
            ],
            axis=dim,
        )
    return cells


def smooth_gate(value):
    return jax.nn.gelu(value, approximate=True)


def on_device(
    saved_conv, grad_out, conv_kernel, weight_in, weight_out, gate_values, picked_slots, slot_counts
):
    frames_dev, rows_dev, grid_cols, local_width = saved_conv.shape
    tokens_dev = frames_dev * rows_dev * grid_cols
    experts_all = weight_in.shape[0]
    slot_size = picked_slots.shape[3]
    flat_conv = saved_conv.reshape(tokens_dev, local_width)
    flat_grad = grad_out.reshape(tokens_dev, local_width)
    slot_index = picked_slots.reshape(experts_all * slot_size)
    slot_live = (
        jnp.arange(slot_size, dtype=jnp.int32)[None, :] < slot_counts.reshape(experts_all, 1)
    ).reshape(-1)
    selector = (
        (slot_index[:, None] == jnp.arange(tokens_dev, dtype=jnp.int32)[None, :])
        & slot_live[:, None]
    ).astype(jnp.bfloat16)
    rows_conv = jnp.dot(selector, flat_conv, preferred_element_type=jnp.float32).astype(
        jnp.bfloat16
    )
    rows_grad = jnp.dot(selector, flat_grad, preferred_element_type=jnp.float32).astype(
        jnp.bfloat16
    )
    rows_conv = rows_conv.reshape(experts_all, slot_size, local_width)
    rows_grad = rows_grad.reshape(experts_all, slot_size, local_width)
    every_conv, every_grad = (
        lax.all_gather(rows_conv, "height", axis=1, tiled=True),
        lax.all_gather(rows_grad, "height", axis=1, tiled=True),
    )
    gate_rows = gate_values.reshape(experts_all, -1)
    pre_part = jnp.einsum("ecd,edk->eck", every_conv, weight_in, preferred_element_type=jnp.float32)
    back_part = jnp.einsum(
        "ecd,ekd->eck", every_grad, weight_out, preferred_element_type=jnp.float32
    )
    pre_full, back_full = lax.psum((pre_part, back_part), "expert")
    activated = smooth_gate(pre_full).astype(jnp.bfloat16)
    _, pullback = jax.vjp(smooth_gate, pre_full)
    grad_pre = pullback(gate_rows[:, :, None] * back_full)[0].astype(jnp.bfloat16)
    scaled_grad = (gate_rows[:, :, None] * every_grad.astype(jnp.float32)).astype(jnp.bfloat16)
    out_part = jnp.einsum(
        "eck,ecd->ekd", activated, scaled_grad, preferred_element_type=jnp.float32
    )
    in_part = jnp.einsum("ecd,eck->edk", every_conv, grad_pre, preferred_element_type=jnp.float32)
    grad_weight_in, grad_weight_out = (
        lax.psum_scatter(
            in_part.astype(jnp.bfloat16).astype(jnp.float32).astype(jnp.bfloat16),
            "tm",
            scatter_dimension=0,
            tiled=True,
        ).astype(jnp.float32),
        lax.psum_scatter(
            out_part.astype(jnp.bfloat16).astype(jnp.float32).astype(jnp.bfloat16),
            "tm",
            scatter_dimension=0,
            tiled=True,
        ).astype(jnp.float32),
    )
    row_terms = jnp.einsum("eck,edk->ecd", grad_pre, weight_in, preferred_element_type=jnp.float32)
    own_rows = lax.psum_scatter(row_terms, "height", scatter_dimension=1, tiled=True).astype(
        jnp.bfloat16
    )
    added = lax.dot_general(
        selector,
        own_rows.reshape(experts_all * slot_size, local_width),
        (((0,), (0,)), ((), ())),
        preferred_element_type=jnp.float32,
    )
    field = (flat_grad.astype(jnp.float32) + added).reshape(
        frames_dev, rows_dev, grid_cols, local_width
    )
    rimmed = extended(field.astype(jnp.bfloat16), (("tm", 0), ("height", 1)), 1)
    padded = jnp.pad(rimmed, ((0, 0), (0, 0), (1, 1), (0, 0)))
    total = field
    for offset_f in range(3):
        for offset_r in range(3):
            for offset_c in range(3):
                kernel_row = conv_kernel[offset_f * 9 + offset_r * 3 + offset_c]
                window = padded[
                    2 - offset_f : 2 - offset_f + frames_dev,
                    2 - offset_r : 2 - offset_r + rows_dev,
                    2 - offset_c : 2 - offset_c + grid_cols,
                ]
                total = total + kernel_row * window.astype(jnp.float32)
    return (total, grad_weight_in, grad_weight_out)


def solution(mesh):
    placed = (
        P("tm", "height", None, "expert"),
        P("tm", "height", None, "expert"),
        P(None, "expert"),
        P(None, "expert", "height"),
        P(None, "height", "expert"),
        P("tm", None, None),
        P("tm", "height", None, None),
        P("tm", "height", None),
    )
    return jax.shard_map(
        on_device,
        mesh=mesh,
        in_specs=placed,
        out_specs=(
            P("tm", "height", None, "expert"),
            P("tm", "expert", "height"),
            P("tm", "height", "expert"),
        ),
        check_vma=False,
    )
```

profile of v0, /device:TPU:1, one launch (start us, length us, event | category | flops | bytes accessed | tf_op | source)
XLA Modules:
  0.0 386.2 jit_solution(11883721412460568624)
XLA Ops:
  7.2 0.0 copy-start
  7.2 0.0 all-gather.3.cloned.1.call-start
  7.2 0.8 eq.15
  8.1 0.7 iota_compare_fusion.3
  8.8 0.1 lt.26
  8.9 1.8 convolution_convert_fusion.2
  10.7 0.0 all-gather.3.cloned.1.call-update
  10.8 0.0 all-gather.5.cloned.1.call-start
  10.8 1.8 convolution_convert_fusion.1
  12.6 0.0 all-gather.5.cloned.1.call-update
  12.7 0.0 all-reduce.4.cloned.1.call-start
  12.7 58.0 %all-gather.3.cloned.1.call-done = bf16[8,256,512]{2,1,0:T(8,128)(2,1)} async-done(((bf16[8,16,512]{2,1,0:T(8,128)(2,1)}), bf16[8,256,512]{2,1,0:T(8,128)(2,1)}) %all-gather.3.cloned.1.call-update) | async-done | bytes 2097168 | tf_op jit(solution)/shard_map/all_gather | solution.py:55
  70.8 3.5 fusion.37
  74.3 44.2 %all-gather.5.cloned.1.call-done = bf16[8,256,512]{2,1,0:T(8,128)(2,1)} async-done(((bf16[8,16,512]{2,1,0:T(8,128)(2,1)}), bf16[8,256,512]{2,1,0:T(8,128)(2,1)}) %all-gather.5.cloned.1.call-update) | async-done | bytes 2097168 | tf_op jit(solution)/shard_map/all_gather | solution.py:54
  118.5 0.0 copy-done
  118.5 3.3 fusion.38
  121.8 0.0 copy-start.5
  121.8 0.0 all-reduce.4.cloned.1.call-update
  121.8 0.0 reduce-scatter.4.cloned.1.call-start
  121.8 87.5 %all-reduce.4.cloned.1.call-done = (f32[8,256,128]{2,1,0:T(8,128)}, f32[8,256,128]{2,1,0:T(8,128)}) async-done(((f32[8,256,128]{2,1,0:T(8,128)}, f32[8,256,128]{2,1,0:T(8,128)}), (f32[8,256,128]{2,1,0:T(8,128)}, f32[8,256,128]{2,1,0:T(8,128)})) %all-reduce.4.cloned.1.call-update) | async-done | bytes 2097168 | tf_op jit(solution)/shard_map/psum | solution.py:62
  209.3 0.0 copy-done.5
  209.3 2.3 fusion.10
  211.6 0.0 copy-start.2
  211.6 0.8 copy-done.2
  212.4 2.6 fusion.39
  215.1 0.0 reduce-scatter.4.cloned.1.call-update
  215.1 0.0 copy-start.1
  215.1 0.0 reduce-scatter.8.cloned.1.call-start
  215.2 4.2 %fusion.3 = bf16[8,128,512]{2,1,0:T(8,128)(2,1)} fusion(bf16[8,256,512]{2,1,0:T(8,128)(2,1)} %all-gather.3.cloned.1.call-done, f32[8,256]{1,0:T(8,128)S(1)} %bitcast.57, f32[8,256,128]{2,1,0:T(8,128)} %get-tuple-element.3), kind=kOutput, calls=%fused_computation.8 | convolution fusion | flops 274464768 | bytes 4202496 | tf_op jit(solution)/shard_map/eck,ecd->ekd/dot_general | solution.py:67
  219.3 0.0 reduce-scatter.8.cloned.1.call-update
  219.3 0.0 copy-start.3
  219.4 0.0 reduce-scatter.6.cloned.1.call-start
  219.4 0.0 copy-done.1
  219.4 2.9 convolution_convert_fusion
  222.3 0.0 copy-start.4
  222.3 0.0 reduce-scatter.6.cloned.1.call-update
  222.3 63.1 %reduce-scatter.4.cloned.1.call-done = f32[8,16,512]{2,1,0:T(8,128)} async-done(((f32[8,256,512]{2,1,0:T(8,128)}), f32[8,16,512]{2,1,0:T(8,128)}) %reduce-scatter.4.cloned.1.call-update) | async-done | bytes 262160 | tf_op jit(solution)/shard_map/reduce_scatter | solution.py:86
  285.5 1.0 convert_element_type.131
  286.4 0.0 copy-done.3
  286.4 0.3 convolution_add_fusion
  286.8 2.8 collective-permute-start
  289.6 1.3 collective-permute-start.1
  290.9 0.0 copy-done.4
  291.0 0.0 collective-permute-done
  291.0 3.7 collective-permute-done.1
  294.7 5.0 %collective-permute-start.2 = (bf16[6,1,16,512]{3,2,1,0:T(8,128)(2,1)S(1)}, bf16[6,1,16,512]{3,2,1,0:T(8,128)(2,1)S(1)}, u32[]{:S(2)}, u32[]{:S(2)}) collective-permute-start(bf16[6,1,16,512]{3,2,1,0:T(8,128)(2,1)S(1)} %get-tuple-element.7), channel_id=1, source_target_pairs={{0,8},{8,16},{16,24},{24,32},{32,40},{40,48},{48,56},{56,64},{64,7... | collective-permute-start | bytes 294920 | tf_op jit(solution)/shard_map/ppermute | solution.py:15
  299.6 3.4 collective-permute-start.3
  303.1 24.6 %reduce-scatter.8.cloned.1.call-done = bf16[1,128,512]{2,1,0:T(8,128)(2,1)} async-done(((bf16[8,128,512]{2,1,0:T(8,128)(2,1)}), bf16[1,128,512]{2,1,0:T(8,128)(2,1)}) %reduce-scatter.8.cloned.1.call-update) | async-done | bytes 131088 | tf_op jit(solution)/shard_map/reduce_scatter | solution.py:78
  327.7 1.6 convert_element_type.166
  329.4 45.1 %reduce-scatter.6.cloned.1.call-done = bf16[1,512,128]{2,1,0:T(8,128)(2,1)} async-done(((bf16[8,512,128]{2,1,0:T(8,128)(2,1)}), bf16[1,512,128]{2,1,0:T(8,128)(2,1)}) %reduce-scatter.6.cloned.1.call-update) | async-done | bytes 131088 | tf_op jit(solution)/shard_map/reduce_scatter | solution.py:72
  374.4 1.6 convert_element_type.161
  376.1 0.0 collective-permute-done.2
  376.1 0.0 collective-permute-done.3
  376.1 0.4 select_maximum_fusion
  376.5 0.1 pad_maximum_fusion
  376.6 2.8 multiply_add_fusion
  (5 shorter events, 0.1 us)
Async XLA Ops:
  7.2 111.3 %copy-start = (bf16[8,512,128]{2,1,0:T(8,128)(2,1)S(1)}, bf16[8,512,128]{2,1,0:T(8,128)(2,1)}, u32[]{:S(2)}) copy-start(bf16[8,512,128]{2,1,0:T(8,128)(2,1)} %param.11) | copy-start | bytes 3145732
  7.2 63.6 %all-gather.3.cloned.1.call-start = ((), (), s32[]{:S(2)}) async-start(), calls=%async_computation.3 | async-start | bytes 2228224 | tf_op jit(solution)/shard_map/all_gather | solution.py:55
  10.8 107.7 %all-gather.5.cloned.1.call-start = ((), (), s32[]{:S(2)}) async-start(), calls=%async_computation.4 | async-start | bytes 2228224 | tf_op jit(solution)/shard_map/all_gather | solution.py:54
  12.7 196.7 %all-reduce.4.cloned.1.call-start = ((), (), s32[]{:S(2)}) async-start(), calls=%async_computation.8 | async-start | bytes 4194304 | tf_op jit(solution)/shard_map/psum | solution.py:62
  121.8 87.6 %copy-start.5 = (f32[1,8,256]{2,1,0:T(8,128)S(1)}, f32[1,8,256]{2,1,0:T(8,128)}, u32[]{:S(2)}) copy-start(f32[1,8,256]{2,1,0:T(8,128)} %param.13) | copy-start | bytes 24580
  121.8 163.7 %reduce-scatter.4.cloned.1.call-start = ((), (), s32[]{:S(2)}) async-start(), calls=%async_computation.5 | async-start | bytes 4456448 | tf_op jit(solution)/shard_map/reduce_scatter | solution.py:86
  211.6 0.8 copy-start.2
  215.1 4.3 %copy-start.1 = (bf16[8,256,512]{2,1,0:T(8,128)(2,1)S(1)}, bf16[8,256,512]{2,1,0:T(8,128)(2,1)}, u32[]{:S(2)}) copy-start(bf16[8,256,512]{2,1,0:T(8,128)(2,1)} %all-gather.5.cloned.1.call-done) | copy-start | bytes 6291460
  215.1 112.6 %reduce-scatter.8.cloned.1.call-start = ((), (), s32[]{:S(2)}) async-start(), calls=%async_computation.7 | async-start | bytes 1179648 | tf_op jit(solution)/shard_map/reduce_scatter | solution.py:78
  219.3 67.1 %copy-start.3 = (bf16[4,4,16,512]{3,2,1,0:T(8,128)(2,1)S(1)}, bf16[4,4,16,512]{3,2,1,0:T(8,128)(2,1)}, u32[]{:S(2)}) copy-start(bf16[4,4,16,512]{3,2,1,0:T(8,128)(2,1)} %param.9) | copy-start | bytes 786436
  219.4 155.1 %reduce-scatter.6.cloned.1.call-start = ((), (), s32[]{:S(2)}) async-start(), calls=%async_computation.6 | async-start | bytes 1179648 | tf_op jit(solution)/shard_map/reduce_scatter | solution.py:72
  222.3 68.6 %copy-start.4 = (f32[27,512]{1,0:T(8,128)S(1)}, f32[27,512]{1,0:T(8,128)}, u32[]{:S(2)}) copy-start(f32[27,512]{1,0:T(8,128)} %param.10) | copy-start | bytes 165892
  286.8 4.1 %collective-permute-start = (bf16[1,4,16,512]{3,2,1,0:T(8,128)(2,1)S(1)}, bf16[1,4,16,512]{3,2,1,0:T(8,128)(2,1)S(1)}, u32[]{:S(2)}, u32[]{:S(2)}) collective-permute-start(bf16[1,4,16,512]{3,2,1,0:T(8,128)(2,1)S(1)} %get-tuple-element.9), channel_id=1, source_target_pairs={{0,128},{128,256},{256,384},{384,512},{512,640},{640,768},{768,896... | collective-permute-start | bytes 196616 | tf_op jit(solution)/shard_map/ppermute | solution.py:15
  289.6 5.0 %collective-permute-start.1 = (bf16[1,4,16,512]{3,2,1,0:T(8,128)(2,1)S(1)}, bf16[1,4,16,512]{3,2,1,0:T(8,128)(2,1)S(1)}, u32[]{:S(2)}, u32[]{:S(2)}) collective-permute-start(bf16[1,4,16,512]{3,2,1,0:T(8,128)(2,1)S(1)} %get-tuple-element.10), channel_id=1, source_target_pairs={{128,0},{256,128},{384,256},{512,384},{640,512},{768,640},{896,768... | collective-permute-start | bytes 196616 | tf_op jit(solution)/shard_map/ppermute | solution.py:17
  294.7 81.4 %collective-permute-start.2 = (bf16[6,1,16,512]{3,2,1,0:T(8,128)(2,1)S(1)}, bf16[6,1,16,512]{3,2,1,0:T(8,128)(2,1)S(1)}, u32[]{:S(2)}, u32[]{:S(2)}) collective-permute-start(bf16[6,1,16,512]{3,2,1,0:T(8,128)(2,1)S(1)} %get-tuple-element.7), channel_id=1, source_target_pairs={{0,8},{8,16},{16,24},{24,32},{32,40},{40,48},{48,56},{56,64},{64,7... | collective-permute-start | bytes 294920 | tf_op jit(solution)/shard_map/ppermute | solution.py:15
  299.6 76.4 %collective-permute-start.3 = (bf16[6,1,16,512]{3,2,1,0:T(8,128)(2,1)S(1)}, bf16[6,1,16,512]{3,2,1,0:T(8,128)(2,1)S(1)}, u32[]{:S(2)}, u32[]{:S(2)}) collective-permute-start(bf16[6,1,16,512]{3,2,1,0:T(8,128)(2,1)S(1)} %get-tuple-element.8), channel_id=1, source_target_pairs={{8,0},{16,8},{24,16},{32,24},{40,32},{48,40},{56,48},{64,56},{72,6... | collective-permute-start | bytes 294920 | tf_op jit(solution)/shard_map/ppermute | solution.py:17
Sparse Core Ops, SparseCore 0:
  11.3 59.3 all-gather.2
  74.0 44.3 all-gather.4
  121.9 87.3 all-reduce.3
  215.2 70.1 reduce-scatter.3
  288.7 38.9 reduce-scatter.7
  331.0 43.3 reduce-scatter.5
where the time goes:
time: 391 us; the launch traced here: 386 us
  waiting for transfers between devices  326 us (83%)
  matrix products  20.5 us (5%)
  between operations  14.3 us (4%)
  starting transfers between devices  12.7 us (3%)
  other arithmetic  10.6 us (3%)
    psum x1, waiting for transfers between devices, on_device(): pre_full, back_full = lax.psum((pre_part, back_part), 'expert')  87.5 us
    reduce_scatter x1, waiting for transfers between devices, on_device(): lax.psum_scatter(row_terms, 'height', scatter_dimension=1, tiled=True)  63.1 us
    all_gather x1, waiting for transfers between devices, on_device(): lax.all_gather(rows_grad, 'height', axis=1, tiled=True)  58 us
    reduce_scatter x1, waiting for transfers between devices, on_device(): lax.psum_scatter(in_part.astype(jnp.bfloat16).astype(jnp.float32).astype(...  45.1 us
    all_gather x1, waiting for transfers between devices, on_device(): lax.all_gather(rows_conv, 'height', axis=1, tiled=True)  44.2 us
    reduce_scatter x1, waiting for transfers between devices, on_device(): lax.psum_scatter(out_part.astype(jnp.bfloat16).astype(jnp.float32).astype...  24.6 us
  transfers between devices with their start and end apart: 10, of which 7 were waited for; matrix products, arithmetic and copies ran while one was open for 4% of the time, Pallas kernels for 0%

commit v1 on v0

v1 whole, which is shorter than its diff:
```python
import functools

import jax
import jax.numpy as jnp
from jax import lax
from jax.experimental import pallas as pl
from jax.experimental.pallas import tpu as pltpu
from jax.sharding import PartitionSpec as P

MESH = pl.DeviceIdType.MESH
HALF = jnp.bfloat16
FULL = jnp.float32


def near_first(count):
    order = [0]
    for step in range(1, count // 2):
        order += [step, count - step]
    return order + [count // 2]


def dot_nn(a, b):
    return lax.dot_general(a, b, (((1,), (0,)), ((), ())), preferred_element_type=FULL)


def dot_nt(a, b):
    return lax.dot_general(a, b, (((1,), (1,)), ((), ())), preferred_element_type=FULL)


def dot_tn(a, b):
    return lax.dot_general(a, b, (((0,), (0,)), ((), ())), preferred_element_type=FULL)


def gelu_and_slope(value):
    scale = 0.7978845608028654
    square = value * value
    tanh = jnp.tanh(scale * (value + 0.044715 * value * square))
    half_up = 0.5 * (1.0 + tanh)
    slope = half_up + 0.5 * value * (1.0 - tanh * tanh) * (
        scale * (1.0 + 3.0 * 0.044715 * square)
    )
    return value * half_up, slope


def body(
    nx, nh, ny,
    conv_ref, grad_ref, taps_ref, win_ref, wout_ref, gate_ref, slots_ref, counts_ref,
    out_ref, gin_ref, gout_ref,
    chosen, rows, w_in, w_out, part_to, part_from, hidden, picked,
    sum_to_r, sum_to_l, sum_from_r, sum_from_l, back_to, back_from,
    grads_own, grads_to, grads_from, field, rim, shifted,
    x_send, x_recv, w_own, w_send, w_recv, z_send, z_recv, p_send, p_recv,
    a_send, a_recv, s_send, s_recv, b_send, b_recv, g_send, g_recv, h_send, h_recv,
):
    nz = nh // 2
    x, h, y = lax.axis_index("tm"), lax.axis_index("height"), lax.axis_index("expert")
    tokens, width = conv_ref.shape
    slot = slots_ref.shape[1]
    picks = nx * slot
    units = win_ref.shape[2]
    x_order, z_order = near_first(nx), near_first(nz)
    x_at = {d: i for i, d in enumerate(x_order)}
    z_at = {d: i for i, d in enumerate(z_order)}
    partner = h + 1 - 2 * lax.rem(h, 2)
    right, left = lax.rem(h + 2, nh), lax.rem(h + nh - 2, nh)
    sides = [(a, b) for a in (-1, 0, 1) for b in (-1, 0, 1) if (a, b) != (0, 0)]

    def x_far(d):
        return lax.rem(x + d + nx, nx)

    def y_far(d):
        return lax.rem(y + d + ny, ny)

    def h_far(d):
        return lax.rem(h + d + nh, nh)

    pending = []

    def remote(src, dst, sems_to, sems_from, device):
        copy = pltpu.make_async_remote_copy(
            src_ref=src, dst_ref=dst, send_sem=sems_to, recv_sem=sems_from,
            device_id=device, device_id_type=MESH,
        )
        copy.start()
        pending.append(copy)
        return copy

    peers = [(x_far(d), h, y) for d in range(1, nx)]
    peers += [(x, h, y_far(d)) for d in range(1, ny)]
    peers += [(x, right, y), (x, left, y), (x, partner, y)]
    peers += [(x_far(a), h_far(b), y) for a, b in sides if b != 0]
    barrier = pltpu.get_barrier_semaphore()
    for peer in peers:
        pl.semaphore_signal(barrier, inc=1, device_id=peer, device_id_type=MESH)

    own_weights = [
        pltpu.make_async_copy(win_ref.at[x], w_in.at[:, pl.ds(0, units)], w_own.at[0]),
        pltpu.make_async_copy(wout_ref.at[x], w_out.at[pl.ds(0, units)], w_own.at[1]),
    ]
    for copy in own_weights:
        copy.start()

    lane = lax.broadcasted_iota(jnp.int32, (nx, picks), 1)
    expert_row = lax.broadcasted_iota(jnp.int32, (nx, picks), 0)
    mine = (lane // slot == expert_row).astype(FULL)
    spread_row = lax.broadcasted_iota(jnp.int32, (slot, picks), 0)
    spread_lane = lax.broadcasted_iota(jnp.int32, (slot, picks), 1)
    spread = (lax.rem(spread_lane, slot) == spread_row).astype(FULL)
    index_row = jnp.sum(
        mine * dot_nn(slots_ref[...].astype(FULL), spread), axis=0, keepdims=True
    )
    count_row = dot_nn(counts_ref[...].astype(FULL), mine)
    lane_row = lax.broadcasted_iota(jnp.int32, (1, picks), 1)
    live = lax.rem(lane_row, slot).astype(FULL) < count_row - 0.5
    index_row = jnp.where(live, index_row, -1.0)
    gate_row_at = lax.broadcasted_iota(jnp.int32, (nh * slot, picks), 0)
    gate_lane = lax.broadcasted_iota(jnp.int32, (nh * slot, picks), 1)
    gate_pick = (gate_row_at == h * slot + lax.rem(gate_lane, slot)).astype(FULL)
    gate_row = jnp.sum(
        mine
        * lax.dot_general(
            gate_ref[...], gate_pick, (((1,), (0,)), ((), ())),
            precision=lax.Precision.HIGHEST, preferred_element_type=FULL,
        ),
        axis=0,
        keepdims=True,
    )
    token = lax.broadcasted_iota(jnp.int32, (tokens, picks), 0).astype(FULL)
    selector = (token == index_row).astype(HALF)
    gates = jnp.transpose(jnp.broadcast_to(gate_row, (picks, picks)))
    gates = jnp.concatenate([gates] * (width // picks), axis=1)
    conv_rows = dot_tn(selector, conv_ref[...]).astype(HALF)
    grad_rows = (dot_tn(selector, grad_ref[...]) * gates).astype(HALF)
    chosen[:, 0] = conv_rows.reshape(nx, slot, width)
    chosen[:, 1] = grad_rows.reshape(nx, slot, width)
    rows[0, 0] = chosen[x]

    pl.semaphore_wait(barrier, len(peers))

    x_copies = {}
    for d in x_order[1:]:
        there = x_at[nx - d]
        x_copies[there] = remote(
            chosen.at[x_far(d)], rows.at[0, there], x_send.at[there], x_recv.at[there],
            (x_far(d), h, y),
        )
    weight_copies = [
        remote(win_ref.at[x], w_in.at[:, pl.ds(units, units)], w_send.at[0], w_recv.at[0],
               (x, partner, y)),
        remote(wout_ref.at[x], w_out.at[pl.ds(units, units)], w_send.at[1], w_recv.at[1],
               (x, partner, y)),
    ]

    split = nx // 2
    halves = (pl.ds(0, split), pl.ds(split, split))
    steps = nz // 2
    z_copies = {}

    def z_forward(step, part, way):
        source = (step - 1) if way == 1 else (nz - step + 1) % nz
        target = step if way == 1 else (nz - step) % nz
        key = ((step - 1) * 2 + part) * 2 + way
        z_copies[step, part, way] = remote(
            rows.at[z_at[source], halves[part]], rows.at[z_at[target], halves[part]],
            z_send.at[key], z_recv.at[key], (x, left if way == 1 else right, y),
        )

    def z_goes(step, part, way):
        return step < steps or (step == steps and part == way)

    for part in (0, 1):
        for there in range(part * split, (part + 1) * split):
            if there in x_copies:
                x_copies[there].wait_recv()
        for way in (0, 1):
            if z_goes(1, part, way):
                z_forward(1, part, way)

    for copy in own_weights:
        copy.wait()
    for copy in weight_copies:
        copy.wait_recv()

    p_copies = {}

    def partial_sums(stage, first, last):
        for block in range(first, last):
            conv_block = rows[block, :, 0].reshape(picks, width)
            grad_block = rows[block, :, 1].reshape(picks, width)
            part_to[:, block, 0] = dot_nn(conv_block, w_in[...]).astype(HALF).reshape(
                ny, slot, 2 * units)
            part_to[:, block, 1] = dot_nt(grad_block, w_out[...]).astype(HALF).reshape(
                ny, slot, 2 * units)
        span = pl.ds(first, last - first)
        for d in reversed(near_first(ny)[1:]):
            key = stage * ny + ny - d
            p_copies[stage, ny - d] = remote(
                part_to.at[y_far(d), span], part_from.at[ny - d, span],
                p_send.at[key], p_recv.at[key], (x, h, y_far(d)),
            )

    def own_hidden(stage, first, last):
        span = pl.ds(first, last - first)
        total = part_to[y, span].astype(FULL)
        for d in range(1, ny):
            p_copies[stage, d].wait_recv()
            total = total + part_from[d, span].astype(FULL)
        activated, slope = gelu_and_slope(total[:, 0])
        hidden[span, y, 0] = activated.astype(HALF)
        hidden[span, y, 1] = (slope * total[:, 1]).astype(HALF)

    spans = [(0, 1)] + [(2 * k - 1, 2 * k + 1) for k in range(1, steps)] + [(nz - 1, nz)]
    partial_sums(0, *spans[0])
    for step in range(1, steps + 1):
        for part in (0, 1):
            for way in (0, 1):
                if z_goes(step, part, way):
                    z_copies[step, part, way].wait_recv()
                    if step < steps and z_goes(step + 1, part, way):
                        z_forward(step + 1, part, way)
        partial_sums(step, *spans[step])
        own_hidden(step - 1, *spans[step - 1])
    own_hidden(steps, *spans[steps])

    y_steps = ny // 2
    blocks = (pl.ds(nz // 2, nz - nz // 2), pl.ds(0, nz // 2))
    a_copies = {}

    def a_forward(step, part, way):
        piece = y_far(step - 1) if way == 1 else y_far(1 - step)
        key = ((step - 1) * 2 + part) * 2 + way
        a_copies[step, part, way] = remote(
            hidden.at[blocks[part], piece], hidden.at[blocks[part], piece],
            a_send.at[key], a_recv.at[key], (x, h, y_far(-1) if way == 1 else y_far(1)),
        )

    def a_goes(step, part, way):
        return step < y_steps or (step == y_steps and part == way)

    for part in (0, 1):
        for way in (0, 1):
            if a_goes(1, part, way):
                a_forward(1, part, way)
    for step in range(1, y_steps + 1):
        for part in (0, 1):
            for way in (0, 1):
                if a_goes(step, part, way):
                    a_copies[step, part, way].wait_recv()
                    if step < y_steps and a_goes(step + 1, part, way):
                        a_forward(step + 1, part, way)

    def picked_block(block):
        grad_pre = hidden[block, :, 1].reshape(picks, 2 * units)
        picked[block] = dot_nt(grad_pre, w_in[...])

    middle = picks // 2
    lines = (pl.ds(0, middle), pl.ds(middle, middle))
    stage_to, stage_from = (sum_to_r, sum_to_l), (sum_from_r, sum_from_l)
    s_copies = {}

    def s_add(step, part, way):
        distance = steps + 1 - step
        block = z_at[distance if way == 0 else (nz - distance) % nz]
        total = picked[block, lines[part]]
        if (step - 1, part, way) in s_copies:
            s_copies[step - 1, part, way].wait_recv()
            total = total + stage_from[way][step - 2, lines[part]].astype(FULL)
        stage_to[way][step - 1, lines[part]] = total.astype(HALF)
        key = ((step - 1) * 2 + part) * 2 + way
        s_copies[step, part, way] = remote(
            stage_to[way].at[step - 1, lines[part]], stage_from[way].at[step - 1, lines[part]],
            s_send.at[key], s_recv.at[key], (x, left if way == 1 else right, y),
        )

    def weight_grads_out():
        activated = hidden[:, :, 0].reshape(nz * picks, 2 * units)
        grads = dot_tn(activated, rows[:, :, 1].reshape(nz * picks, width))
        gout_ref[...] = grads[:units]
        grads_to[0] = grads[units:]

    def weight_grads_in():
        grad_pre = hidden[:, :, 1].reshape(nz * picks, 2 * units)
        grads = dot_tn(grad_pre, rows[:, :, 0].reshape(nz * picks, width))
        grads_own[...] = grads[:units]
        grads_to[1] = grads[units:]

    picked_block(nz - 1)
    for way in (0, 1):
        s_add(1, way, way)
    for step in range(2, steps + 1):
        distance = steps + 1 - step
        for block in (z_at[distance], z_at[nz - distance]):
            picked_block(block)
        if step == steps:
            weight_grads_out()
        for part in (0, 1):
            for way in (0, 1):
                s_add(step, part, way)
    picked_block(0)
    for part in (0, 1):
        total = picked[0, lines[part]]
        for way in (0, 1):
            if (steps, part, way) in s_copies:
                s_copies[steps, part, way].wait_recv()
                total = total + stage_from[way][steps - 1, lines[part]].astype(FULL)
        back_to[pl.ds(part * split, split)] = total.astype(HALF).reshape(split, slot, width)

    b_copies = []
    for d in x_order[1:]:
        b_copies.append(
            remote(back_to.at[x_at[d]], back_from.at[x], b_send.at[d], b_recv.at[d],
                   (x_far(d), h, y))
        )
    back_from[x] = back_to[0]
    weight_grads_in()
    g_copy = remote(grads_to, grads_from, g_send, g_recv, (x, partner, y))
    for copy in b_copies:
        copy.wait_recv()
    added = dot_nn(selector, back_from[...].reshape(picks, width))
    total_field = grad_ref[...].astype(FULL) + added
    frames, grid_rows, columns, _ = out_ref.shape
    field[...] = total_field.reshape(frames, grid_rows, columns, width)
    rim[pl.ds(1, frames), pl.ds(1, grid_rows)] = total_field.astype(HALF).reshape(
        frames, grid_rows, columns, width)

    def face(side, size, inside):
        if side == 0:
            return pl.ds(1, size)
        if inside:
            return pl.ds(1 if side < 0 else size, 1)
        return pl.ds(size + 1 if side < 0 else 0, 1)

    h_copies = []
    for at, (a, b) in enumerate(sides):
        h_copies.append(
            remote(
                rim.at[face(a, frames, True), face(b, grid_rows, True)],
                rim.at[face(a, frames, False), face(b, grid_rows, False)],
                h_send.at[at], h_recv.at[at], (x_far(a), h_far(b), y),
            )
        )

    g_copy.wait_recv()
    gout_ref[...] += grads_from[0]
    gin_ref[...] = jnp.transpose(grads_own[...] + grads_from[1])

    for copy in h_copies:
        copy.wait_recv()

    at_column = lax.broadcasted_iota(jnp.int32, (columns, width), 0)

    def shift(cell, _):
        f, r = cell // (grid_rows + 2), lax.rem(cell, grid_rows + 2)
        outside = ((f == 0) & (x == 0)) | ((f == frames + 1) & (x == nx - 1))
        outside |= ((r == 0) & (h == 0)) | ((r == grid_rows + 1) & (h == nh - 1))
        here = jnp.where(outside, 0.0, rim[f, r].astype(FULL))
        shifted[1, f, r] = here
        shifted[0, f, r] = jnp.where(
            at_column == columns - 1, 0.0, pltpu.roll(here, columns - 1, 0))
        shifted[2, f, r] = jnp.where(at_column == 0, 0.0, pltpu.roll(here, 1, 0))
        return _

    lax.fori_loop(0, (frames + 2) * (grid_rows + 2), shift, 0)

    def convolve(f, _):
        total = field[f]
        for a in range(3):
            for b in range(3):
                for k in range(3):
                    tap = taps_ref[pl.ds(9 * a + 3 * b + k, 1)].reshape(1, 1, width)
                    total = total + tap * shifted[k, f + 2 - a, pl.ds(2 - b, grid_rows)]
        out_ref[f] = total
        return _

    lax.fori_loop(0, frames, convolve, 0)

    for copy in pending:
        copy.wait_send()


def on_device(
    nx, nh, ny,
    saved_conv, grad_out, conv_kernel, weight_in, weight_out, gate_values, picked_slots, slot_counts,
):
    nz = nh // 2
    frames, grid_rows, columns, width = saved_conv.shape
    tokens = frames * grid_rows * columns
    experts, _, units = weight_in.shape
    slot = picked_slots.shape[3]
    picks = experts * slot
    vmem = pl.BlockSpec(memory_space=pltpu.VMEM)
    hbm = pl.BlockSpec(memory_space=pl.ANY)
    steps = nz // 2
    dma = pltpu.SemaphoreType.DMA
    out, grad_in, grad_w = pl.pallas_call(
        functools.partial(body, nx, nh, ny),
        out_shape=(
            jax.ShapeDtypeStruct((frames, grid_rows, columns, width), FULL),
            jax.ShapeDtypeStruct((width, units), FULL),
            jax.ShapeDtypeStruct((units, width), FULL),
        ),
        in_specs=[vmem, vmem, vmem, hbm, hbm, vmem, vmem, vmem],
        out_specs=(vmem, vmem, vmem),
        scratch_shapes=[
            pltpu.VMEM((experts, 2, slot, width), HALF),
            pltpu.VMEM((nz, nx, 2, slot, width), HALF),
            pltpu.VMEM((width, 2 * units), HALF),
            pltpu.VMEM((2 * units, width), HALF),
            pltpu.VMEM((ny, nz, 2, slot, 2 * units), HALF),
            pltpu.VMEM((ny, nz, 2, slot, 2 * units), HALF),
            pltpu.VMEM((nz, ny, 2, slot, 2 * units), HALF),
            pltpu.VMEM((nz, picks, width), FULL),
            pltpu.VMEM((steps, picks, width), HALF),
            pltpu.VMEM((steps, picks, width), HALF),
            pltpu.VMEM((steps, picks, width), HALF),
            pltpu.VMEM((steps, picks, width), HALF),
            pltpu.VMEM((nx, slot, width), HALF),
            pltpu.VMEM((nx, slot, width), HALF),
            pltpu.VMEM((units, width), FULL),
            pltpu.VMEM((2, units, width), FULL),
            pltpu.VMEM((2, units, width), FULL),
            pltpu.VMEM((frames, grid_rows, columns, width), FULL),
            pltpu.VMEM((frames + 2, grid_rows + 2, columns, width), HALF),
            pltpu.VMEM((3, frames + 2, grid_rows + 2, columns, width), FULL),
            dma((nx,)), dma((nx,)),
            dma((2,)), dma((2,)), dma((2,)),
            dma((4 * steps,)), dma((4 * steps,)),
            dma(((steps + 1) * ny,)), dma(((steps + 1) * ny,)),
            dma((2 * ny,)), dma((2 * ny,)),
            dma((4 * steps,)), dma((4 * steps,)),
            dma((nx,)), dma((nx,)),
            dma(()), dma(()),
            dma((8,)), dma((8,)),
        ],
        compiler_params=pltpu.CompilerParams(
            collective_id=0, has_side_effects=True, vmem_limit_bytes=48 * 1024 * 1024
        ),
    )(
        saved_conv.reshape(tokens, width),
        grad_out.reshape(tokens, width),
        conv_kernel,
        weight_in,
        weight_out,
        gate_values.reshape(gate_values.shape[1:]),
        picked_slots.reshape(experts, slot),
        slot_counts.reshape(1, experts),
    )
    return out, grad_in[None], grad_w[None]


def solution(mesh):
    placed = (
        P("tm", "height", None, "expert"),
        P("tm", "height", None, "expert"),
        P(None, "expert"),
        P(None, "expert", "height"),
        P(None, "height", "expert"),
        P("tm", None, None),
        P("tm", "height", None, None),
        P("tm", "height", None),
    )
    sizes = (mesh.shape["tm"], mesh.shape["height"], mesh.shape["expert"])
    return jax.shard_map(
        functools.partial(on_device, *sizes),
        mesh=mesh,
        in_specs=placed,
        out_specs=(
            P("tm", "height", None, "expert"),
            P("tm", "expert", "height"),
            P("tm", "height", "expert"),
        ),
        check_vma=False,
    )
```

time: 391 us -> 116 us (0.30); the launches traced: 386 us -> 116 us
  waiting for transfers between devices: 326 us -> 0 us
  Pallas kernels: 0 us -> 106 us
  matrix products: 20.5 us -> 0 us
  between operations: 14.3 us -> 0.67 us
  starting transfers between devices: 12.7 us -> 0 us
  other arithmetic: 10.6 us -> 0 us
  local copies, waits for them, and re-layouts: 1.81 us -> 8.76 us
    reduce_scatter x3 -> x0, waiting for transfers between devices: 133 us -> none  [the longest x1 63.1 us: on_device(): lax.psum_scatter(row_terms, 'height', scatter_dimension=1, tiled=True)]
    pallas_call x0 -> x1, Pallas kernels: none -> 106 us  [on_device(): pl.pallas_call(functools.partial(body, nx, nh, ny), out_shape=(jax.ShapeD...]
    all_gather x2 -> x0, waiting for transfers between devices: 102 us -> none  [the longest x1 58 us: on_device(): lax.all_gather(rows_grad, 'height', axis=1, tiled=True)]
    psum x1 -> x0, waiting for transfers between devices: 87.5 us -> none  [on_device(): pre_full, back_full = lax.psum((pre_part, back_part), 'expert')]
    dot_general x8 -> x0, matrix products: 20.5 us -> none  [the longest x1 4.16 us: on_device(): jnp.einsum('eck,ecd->ekd', activated, scaled_grad, preferred_element_type...]
    ppermute x4 -> x0, starting transfers between devices: 12.5 us -> none  [the longest x2 7.74 us: extended(): lax.ppermute(tail, axis, [(i, (i + 1) % count) for i in range(ends)])]
    unnamed x12 -> x19, local copies, waits for them, and re-layouts: 0.82 us -> 8.76 us
    convert_element_type x5 -> x0, other arithmetic: 6.57 us -> none  [the longest x2 3.26 us: on_device(): grad_weight_in, grad_weight_out = (lax.psum_scatter(in_part.astype(jnp.bf...]
  transfers between devices with their start and end apart: 10 -> 0, of which waited for: 7 -> 0; matrix products, arithmetic and copies ran while one was open for 4% -> 0% of each run, Pallas kernels for 0% -> 0%
where the time goes in v1:
time: 116 us
  Pallas kernels  106 us (91%)
  local copies, waits for them, and re-layouts  8.76 us (8%)
    pallas_call x1, Pallas kernels, on_device(): pl.pallas_call(functools.partial(body, nx, nh, ny), out_shape=(jax.ShapeD...  106 us
    unnamed x19, local copies, waits for them, and re-layouts  8.76 us

profile of v1, /device:TPU:1, one launch (start us, length us, event | category | flops | bytes accessed | tf_op | source)
XLA Modules:
  0.0 115.8 jit_solution(8242966142417702886)
XLA Ops:
  0.6 0.0 copy-start.5
  0.6 0.0 copy-start.7
  0.7 0.7 copy-done.5
  1.3 0.0 copy-done.7
  1.3 0.0 copy-start
  1.3 1.2 %copy-done = bf16[8,512,128]{2,1,0:T(8,128)(2,1)S(1)} copy-done((bf16[8,512,128]{2,1,0:T(8,128)(2,1)S(1)}, bf16[8,512,128]{2,1,0:T(8,128)(2,1)}, u32[]{:S(2)}) %copy-start) | copy-done | bytes 1048600
  2.6 0.0 copy-start.1
  2.6 1.2 %copy-done.1 = bf16[8,128,512]{2,1,0:T(8,128)(2,1)S(1)} copy-done((bf16[8,128,512]{2,1,0:T(8,128)(2,1)S(1)}, bf16[8,128,512]{2,1,0:T(8,128)(2,1)}, u32[]{:S(2)}) %copy-start.1) | copy-done | bytes 1048600
  3.8 0.0 copy-start.2
  3.8 0.9 copy-done.2
  4.7 0.0 copy-start.3
  4.7 0.9 copy-done.3
  5.7 0.0 copy-start.4
  5.7 0.8 copy-done.4
  6.5 0.0 copy-start.6
  6.5 0.7 copy-done.6
  7.2 106.4 %shard_map.103 = (f32[4,4,16,512]{3,2,1,0:T(8,128)S(1)}, f32[512,128]{1,0:T(8,128)S(1)}, f32[128,512]{1,0:T(8,128)S(1)}) custom-call(bf16[256,512]{1,0:T(8,128)(2,1)S(1)} %bitcast.7, bf16[256,512]{1,0:T(8,128)(2,1)S(1)} %bitcast.8, f32[27,512]{1,0:T(8,128)S(1)} %copy-done.4, bf16[8,512,128]{2,1,0:T(8,128)(2,1)S(1)} %copy-done, ...), custom_call_target="tpu_custom_call" | custom-call | tf_op jit(solution)/shard_map/pallas_call | solution.py:395
  113.6 0.8 copy.14
  114.4 0.7 copy.15
  115.1 0.7 copy.16
Async XLA Ops:
  0.6 0.7 copy-start.5
  0.6 0.7 copy-start.7
  1.3 1.2 %copy-start = (bf16[8,512,128]{2,1,0:T(8,128)(2,1)S(1)}, bf16[8,512,128]{2,1,0:T(8,128)(2,1)}, u32[]{:S(2)}) copy-start(bf16[8,512,128]{2,1,0:T(8,128)(2,1)} %win_ref.1) | copy-start | bytes 3145732
  2.6 1.2 %copy-start.1 = (bf16[8,128,512]{2,1,0:T(8,128)(2,1)S(1)}, bf16[8,128,512]{2,1,0:T(8,128)(2,1)}, u32[]{:S(2)}) copy-start(bf16[8,128,512]{2,1,0:T(8,128)(2,1)} %wout_ref.1) | copy-start | bytes 3145732
  3.8 0.9 copy-start.2
  4.7 0.9 copy-start.3
  5.7 0.8 copy-start.4
  6.5 0.7 copy-start.6

commit v2 on v1

v2 whole, which is shorter than its diff:
```python
import functools

import jax
import jax.numpy as jnp
from jax import lax
from jax.experimental import pallas as pl
from jax.experimental.pallas import tpu as pltpu
from jax.sharding import PartitionSpec as P

MESH = pl.DeviceIdType.MESH
HALF = jnp.bfloat16
FULL = jnp.float32


def near_first(count):
    order = [0]
    for step in range(1, count // 2):
        order += [step, count - step]
    return order + [count // 2]


def dot_nn(a, b):
    return lax.dot_general(a, b, (((1,), (0,)), ((), ())), preferred_element_type=FULL)


def dot_nt(a, b):
    return lax.dot_general(a, b, (((1,), (1,)), ((), ())), preferred_element_type=FULL)


def dot_tn(a, b):
    return lax.dot_general(a, b, (((0,), (0,)), ((), ())), preferred_element_type=FULL)


def gelu_and_slope(value):
    scale = 0.7978845608028654
    square = value * value
    tanh = jnp.tanh(scale * (value + 0.044715 * value * square))
    half_up = 0.5 * (1.0 + tanh)
    slope = half_up + 0.5 * value * (1.0 - tanh * tanh) * (
        scale * (1.0 + 3.0 * 0.044715 * square)
    )
    return value * half_up, slope


def body(
    nx, nh, ny,
    conv_hbm, grad_hbm, taps_hbm, win_ref, wout_ref, gate_hbm, slots_hbm, counts_hbm,
    out_ref, gin_ref, gout_ref,
    conv_ref, grad_ref, taps_ref, gate_ref, slots_ref, counts_ref, chosen,
    rows, w_in, w_out, part_to, part_from, relay, hidden, hidden_own, pre_grads, back_to, back_from,
    grads_own, grads_to, grads_from, field, rim, shifted,
    i_own, x_send, x_recv, w_own, w_send, w_recv, v_send, v_recv, u_send, u_recv,
    z_send, z_recv, p_send, p_recv, c_send, c_recv, e_send, e_recv,
    a_send, a_recv, b_send, b_recv, g_send, g_recv, h_send, h_recv,
):
    nz = nh // 2
    x, h, y = lax.axis_index("tm"), lax.axis_index("height"), lax.axis_index("expert")
    tokens, width = conv_ref.shape
    slot = slots_ref.shape[1]
    picks = nx * slot
    units = win_ref.shape[2]
    x_order, z_order = near_first(nx), near_first(nz)
    x_at = {d: i for i, d in enumerate(x_order)}
    z_at = {d: i for i, d in enumerate(z_order)}
    partner = h + 1 - 2 * lax.rem(h, 2)
    sides = [(a, b) for a in (-1, 0, 1) for b in (-1, 0, 1) if (a, b) != (0, 0)]
    steps = nz // 2
    spans = [(0, 3)] + [(2 * k - 1, 2 * k + 1) for k in range(2, steps)] + [(nz - 1, nz)]
    last_stage = len(spans) - 1
    relayed = last_stage - 1 if ny == 8 else 0

    def x_far(d):
        return lax.rem(x + d + nx, nx)

    def y_far(d):
        return lax.rem(y + d + ny, ny)

    def h_far(d):
        return lax.rem(h + d + nh, nh)

    def z_far(d):
        return lax.rem(h + 2 * d + nh, nh)

    def onward(way):
        return (x, z_far(-1 if way else 1), y)

    pending = []

    def remote(src, dst, sems_to, sems_from, device):
        copy = pltpu.make_async_remote_copy(
            src_ref=src, dst_ref=dst, send_sem=sems_to, recv_sem=sems_from,
            device_id=device, device_id_type=MESH,
        )
        copy.start()
        pending.append(copy)
        return copy

    peers = [(x_far(d), h, y) for d in range(1, nx)]
    peers += [(x, h, y_far(d)) for d in range(1, ny)]
    peers += [(x, z_far(d), y) for d in range(1, nz)]
    peers += [(x, partner, y)]
    peers += [(x_far(a), h_far(b), y) for a, b in sides if b != 0]
    barrier = pltpu.get_barrier_semaphore()
    for peer in peers:
        pl.semaphore_signal(barrier, inc=1, device_id=peer, device_id_type=MESH)

    own, other = pl.ds(0, units), pl.ds(units, units)
    inputs = [
        pltpu.make_async_copy(src, dst, i_own.at[at])
        for at, (src, dst) in enumerate(
            [
                (slots_hbm, slots_ref), (counts_hbm, counts_ref), (gate_hbm, gate_ref),
                (conv_hbm, conv_ref), (grad_hbm, grad_ref), (taps_hbm, taps_ref),
            ]
        )
    ]
    own_weights = [
        pltpu.make_async_copy(win_ref.at[x], w_in.at[0, :, own], w_own.at[0]),
        pltpu.make_async_copy(wout_ref.at[x], w_out.at[0, own], w_own.at[1]),
    ]
    for copy in inputs + own_weights:
        copy.start()

    lane = lax.broadcasted_iota(jnp.int32, (nx, picks), 1)
    expert_row = lax.broadcasted_iota(jnp.int32, (nx, picks), 0)
    mine = (lane // slot == expert_row).astype(FULL)
    spread_row = lax.broadcasted_iota(jnp.int32, (slot, picks), 0)
    spread_lane = lax.broadcasted_iota(jnp.int32, (slot, picks), 1)
    spread = (lax.rem(spread_lane, slot) == spread_row).astype(FULL)
    gate_row_at = lax.broadcasted_iota(jnp.int32, (nh * slot, picks), 0)
    gate_lane = lax.broadcasted_iota(jnp.int32, (nh * slot, picks), 1)
    gate_pick = (gate_row_at == h * slot + lax.rem(gate_lane, slot)).astype(FULL)
    token = lax.broadcasted_iota(jnp.int32, (tokens, picks), 0).astype(FULL)
    lane_row = lax.broadcasted_iota(jnp.int32, (1, picks), 1)
    for copy in inputs:
        copy.wait()
    index_row = jnp.sum(
        mine * dot_nn(slots_ref[...].astype(FULL), spread), axis=0, keepdims=True
    )
    count_row = dot_nn(counts_ref[...].astype(FULL), mine)
    live = lax.rem(lane_row, slot).astype(FULL) < count_row - 0.5
    index_row = jnp.where(live, index_row, -1.0)
    gate_row = jnp.sum(
        mine
        * lax.dot_general(
            gate_ref[...], gate_pick, (((1,), (0,)), ((), ())),
            precision=lax.Precision.HIGHEST, preferred_element_type=FULL,
        ),
        axis=0,
        keepdims=True,
    )
    selector = (token == index_row).astype(HALF)
    gates = jnp.transpose(jnp.broadcast_to(gate_row, (picks, picks)))
    gates = jnp.concatenate([gates] * (width // picks), axis=1)
    conv_rows = dot_tn(selector, conv_ref[...]).astype(HALF)
    grad_rows = (dot_tn(selector, grad_ref[...]) * gates).astype(HALF)
    chosen[:, 0] = conv_rows.reshape(nx, slot, width)
    chosen[:, 1] = grad_rows.reshape(nx, slot, width)
    rows[0, 0] = chosen[x]

    pl.semaphore_wait(barrier, len(peers))

    x_copies = {}
    for d in x_order[1:]:
        there = x_at[nx - d]
        x_copies[there] = remote(
            chosen.at[x_far(d)], rows.at[0, there], x_send.at[there], x_recv.at[there],
            (x_far(d), h, y),
        )
    weight_copies = [
        remote(win_ref.at[x], w_in.at[0, :, other], w_send.at[0], w_recv.at[0],
               (x, partner, y)),
        remote(wout_ref.at[x], w_out.at[0, other], w_send.at[1], w_recv.at[1],
               (x, partner, y)),
    ]

    v_copies, u_copies = {}, {}

    def v_block(step, way):
        return z_at[(step if way else nz - step) % nz]

    def v_half(block, part, half):
        return w_out.at[block, half] if part else w_in.at[block, :, half]

    def v_goes(step, part, way):
        return step < steps or (step == steps and part == way)

    def v_forward(step, part, way):
        key = ((step - 1) * 2 + part) * 2 + way
        if step == 1:
            source = (wout_ref if part else win_ref).at[x]
        else:
            source = v_half(v_block(step - 1, way), part, own)
        v_copies[step, part, way] = remote(
            source, v_half(v_block(step, way), part, own), v_send.at[key], v_recv.at[key],
            onward(way),
        )

    def v_arrive(step):
        for part in (0, 1):
            for way in (0, 1):
                if v_goes(step, part, way):
                    v_copies[step, part, way].wait_recv()
                    if step < steps and v_goes(step + 1, part, way):
                        v_forward(step + 1, part, way)
                    block, key = v_block(step, way), ((step - 1) * 2 + part) * 2 + way
                    u_copies[step, part, way] = remote(
                        v_half(block, part, own), v_half(block, part, other),
                        u_send.at[key], u_recv.at[key], (x, partner, y),
                    )

    parts = min(2, nx)
    split = nx // parts
    z_copies = {}

    def z_forward(step, part, way):
        source = (step - 1) if way == 1 else (nz - step + 1) % nz
        target = step if way == 1 else (nz - step) % nz
        key = ((step - 1) * parts + part) * 2 + way
        groups = pl.ds(part * split, split)
        z_copies[step, part, way] = remote(
            rows.at[z_at[source], groups], rows.at[z_at[target], groups],
            z_send.at[key], z_recv.at[key], onward(way),
        )

    def z_goes(step, part, way):
        return step < steps or (step == steps and (2 * part // parts) == way)

    def z_start():
        for part in range(parts):
            for way in (0, 1):
                if z_goes(1, part, way):
                    z_forward(1, part, way)

    def z_arrive(step):
        if step > steps:
            return
        for part in range(parts):
            for way in (0, 1):
                if z_goes(step, part, way):
                    z_copies[step, part, way].wait_recv()
                    if step < steps and z_goes(step + 1, part, way):
                        z_forward(step + 1, part, way)

    p_copies, c_copies, e_copies = {}, {}, {}

    def p_send_to(stage, at, source, target, distance):
        key = stage * ny + at
        p_copies[stage, at] = remote(
            source, target, p_send.at[key], p_recv.at[key], (x, h, y_far(distance)))

    def e_send_to(stage, at, piece, distance):
        key = stage * ny + at
        e_copies[stage, at] = remote(
            piece, piece, e_send.at[key], e_recv.at[key], (x, h, y_far(distance)))

    def cut(stage):
        first, last = spans[stage]
        middle = first + (last - first + 1) // 2
        return first, middle, last

    def partial_sums(stage):
        first, middle, last = cut(stage)
        for part in (0, 1):
            for way in (0, 1):
                for step in ([1] if stage == 0 else [stage + 1]):
                    if (step, part, way) in u_copies:
                        u_copies[step, part, way].wait_recv()
        conv_block = rows[0, :, 0].reshape(picks, width)
        grad_block = rows[0, :, 1].reshape(picks, width)
        for block in range(first, last):
            part_to[:, block, 0] = dot_nn(conv_block, w_in[block]).astype(HALF).reshape(
                ny, slot, 2 * units)
            part_to[:, block, 1] = dot_nt(grad_block, w_out[block]).astype(HALF).reshape(
                ny, slot, 2 * units)
        span = pl.ds(first, last - first)
        if stage >= relayed:
            for d in reversed(near_first(ny)[1:]):
                p_send_to(stage, ny - d, part_to.at[y_far(d), span],
                          part_from.at[ny - d, span], d)
            return
        for way in (1, -1):
            p_send_to(stage, 4 - way, part_to.at[y_far(-3 * way), span],
                      part_from.at[4 - way, span], -way)
        for way, lines in ((1, pl.ds(first, middle - first)), (-1, pl.ds(middle, last - middle))):
            p_send_to(stage, 4 if way == 1 else 0, part_to.at[y_far(4), lines],
                      part_from.at[4, lines], -2 * way)
        for way in (1, -1):
            p_send_to(stage, 4 - 3 * way, part_to.at[y_far(-way), span],
                      part_from.at[4 - 3 * way, span], -way)

    def relay_sums(stage):
        if stage >= relayed:
            return
        first, middle, last = cut(stage)
        span = pl.ds(first, last - first)
        for way, start, stop in ((1, first, middle), (-1, middle, last)):
            p_copies[stage, 4 - way].wait_recv()
            p_copies[stage, 4 if way == 1 else 0].wait_recv()
            lines = pl.ds(start, stop - start)
            relay[int(way > 0), span] = (
                part_to[y_far(-2 * way), span].astype(FULL)
                + part_from[4 - way, span].astype(FULL)
            ).astype(HALF)
            relay[int(way > 0), lines] = (
                part_to[y_far(-2 * way), lines].astype(FULL)
                + part_from[4 - way, lines].astype(FULL)
                + part_from[4, lines].astype(FULL)
            ).astype(HALF)
            p_send_to(stage, 4 - 2 * way, relay.at[int(way > 0), span],
                      part_from.at[4 - 2 * way, span], -2 * way)

    def own_hidden(stage):
        first, middle, last = cut(stage)
        span = pl.ds(first, last - first)
        total = part_to[y, span].astype(FULL)
        for d in ((1, 7, 2, 6) if stage < relayed else range(1, ny)):
            p_copies[stage, d].wait_recv()
            total = total + part_from[d, span].astype(FULL)
        activated, slope = gelu_and_slope(total[:, 0])
        grad_pre = (slope * total[:, 1]).astype(HALF)
        pre_grads[span, y] = grad_pre
        piece = pre_grads.at[span, y]
        if stage < relayed:
            for d in (2, 6, 1, 7):
                e_send_to(stage, ny - d, piece, d)
        else:
            for d in reversed(near_first(ny)[1:]):
                e_send_to(stage, ny - d, piece, d)
        hidden_own[span, 0] = activated.astype(HALF)
        hidden_own[span, 1] = grad_pre
        for block in range(first, last):
            distance = z_order[block]
            if distance == 0:
                hidden[0, y] = hidden_own[0]
                continue
            there = z_at[nz - distance]
            c_copies[there] = remote(
                hidden_own.at[block], hidden.at[there, y], c_send.at[there], c_recv.at[there],
                (x, z_far(distance), y),
            )

    def relay_grads(stage):
        if stage >= relayed:
            return
        first, middle, last = cut(stage)
        span = pl.ds(first, last - first)
        for way, lines in ((1, pl.ds(first, middle - first)), (-1, pl.ds(middle, last - middle))):
            e_copies[stage, 4 + 2 * way].wait_recv()
            source = y_far(-2 * way)
            e_send_to(stage, 4 + way, pre_grads.at[span, source], way)
            e_send_to(stage, 4 if way == 1 else 0, pre_grads.at[lines, source], 2 * way)

    for part in (0, 1):
        for way in (0, 1):
            if v_goes(1, part, way):
                v_forward(1, part, way)
    v_arrive(1)
    for copy in x_copies.values():
        copy.wait_recv()
    for copy in own_weights:
        copy.wait()
    for copy in weight_copies:
        copy.wait_recv()
    partial_sums(0)
    for stage in range(1, last_stage + 1):
        v_arrive(stage + 1)
        if stage == max(last_stage - 1, 1):
            z_start()
        partial_sums(stage)
        relay_sums(stage - 1)
        if stage >= 2:
            own_hidden(stage - 2)
    if last_stage >= 1:
        own_hidden(last_stage - 1)

    y_steps = ny // 2
    bound = spans[max(last_stage - 2, 0)][1]
    blocks = (pl.ds(0, bound), pl.ds(bound, nz - bound))
    a_copies = {}

    def a_forward(step, part, way):
        piece = y_far(step - 1) if way == 1 else y_far(1 - step)
        key = ((step - 1) * 2 + part) * 2 + way
        a_copies[step, part, way] = remote(
            hidden.at[blocks[part], piece], hidden.at[blocks[part], piece],
            a_send.at[key], a_recv.at[key], (x, h, y_far(-1) if way == 1 else y_far(1)),
        )

    def a_goes(step, part, way):
        return step < y_steps or (step == y_steps and part == way)

    def a_start(part):
        for block in range(nz):
            if (block < bound) == (part == 0) and block in c_copies:
                c_copies[block].wait_recv()
        for way in (0, 1):
            if a_goes(1, part, way):
                a_forward(1, part, way)

    def a_arrive(step, part):
        if step > y_steps:
            return
        for way in (0, 1):
            if a_goes(step, part, way):
                a_copies[step, part, way].wait_recv()
                if step < y_steps and a_goes(step + 1, part, way):
                    a_forward(step + 1, part, way)

    for stage in range(last_stage - 1):
        relay_grads(stage)
    z_arrive(1)
    a_start(0)
    own_hidden(last_stage)
    z_arrive(2)
    a_start(1)
    a_arrive(1, 0)

    total = jnp.zeros((picks, width), FULL)
    for stage in range(last_stage + 1):
        for d in range(ny):
            if (stage, d) in e_copies and not (stage < relayed and d in (2, 6)):
                e_copies[stage, d].wait_recv()
        for block in range(*spans[stage]):
            total += dot_nt(pre_grads[block].reshape(picks, 2 * units), w_in[block])
    back_to[...] = total.astype(HALF).reshape(nx, slot, width)

    b_copies = []
    for d in x_order[1:]:
        b_copies.append(
            remote(back_to.at[x_at[d]], back_from.at[x], b_send.at[d], b_recv.at[d],
                   (x_far(d), h, y))
        )
    back_from[x] = back_to[0]
    a_arrive(1, 1)
    a_arrive(2, 0)
    z_arrive(3)
    for copy in b_copies:
        copy.wait_recv()
    added = dot_nn(selector, back_from[...].reshape(picks, width))
    total_field = grad_ref[...].astype(FULL) + added
    frames, grid_rows, columns, _ = out_ref.shape
    rim[pl.ds(1, frames), pl.ds(1, grid_rows)] = total_field.astype(HALF).reshape(
        frames, grid_rows, columns, width)

    def face(side, size, inside):
        if side == 0:
            return pl.ds(1, size)
        if inside:
            return pl.ds(1 if side < 0 else size, 1)
        return pl.ds(size + 1 if side < 0 else 0, 1)

    h_copies = []
    for at, (a, b) in enumerate(sides):
        h_copies.append(
            remote(
                rim.at[face(a, frames, True), face(b, grid_rows, True)],
                rim.at[face(a, frames, False), face(b, grid_rows, False)],
                h_send.at[at], h_recv.at[at], (x_far(a), h_far(b), y),
            )
        )
    field[...] = total_field.reshape(frames, grid_rows, columns, width)
    a_arrive(2, 1)
    a_arrive(3, 0)

    at_column = lax.broadcasted_iota(jnp.int32, (columns, width), 0)

    def shift_cell(f, r, here):
        shifted[1, f, r] = here
        shifted[0, f, r] = jnp.where(
            at_column == columns - 1, 0.0, pltpu.roll(here, columns - 1, 0))
        shifted[2, f, r] = jnp.where(at_column == 0, 0.0, pltpu.roll(here, 1, 0))

    def shift_inner(cell, _):
        f, r = 1 + cell // grid_rows, 1 + lax.rem(cell, grid_rows)
        shift_cell(f, r, rim[f, r].astype(FULL))
        return _

    lax.fori_loop(0, frames * grid_rows, shift_inner, 0)
    a_arrive(3, 1)
    for copy in h_copies:
        copy.wait_recv()

    def shift_outer(cell, f, r):
        outside = ((f == 0) & (x == 0)) | ((f == frames + 1) & (x == nx - 1))
        outside |= ((r == 0) & (h == 0)) | ((r == grid_rows + 1) & (h == nh - 1))
        shift_cell(f, r, jnp.where(outside, 0.0, rim[f, r].astype(FULL)))
        return cell

    def shift_ends(cell, _):
        return shift_outer(
            _, (cell // (grid_rows + 2)) * (frames + 1), lax.rem(cell, grid_rows + 2))

    def shift_sides(cell, _):
        return shift_outer(_, 1 + cell // 2, lax.rem(cell, 2) * (grid_rows + 1))

    lax.fori_loop(0, 2 * (grid_rows + 2), shift_ends, 0)
    lax.fori_loop(0, 2 * frames, shift_sides, 0)

    def convolve(f, _):
        total = field[f]
        for a in range(3):
            for b in range(3):
                for k in range(3):
                    tap = taps_ref[pl.ds(9 * a + 3 * b + k, 1)].reshape(1, 1, width)
                    total = total + tap * shifted[k, f + 2 - a, pl.ds(2 - b, grid_rows)]
        out_ref[f] = total
        return _

    lax.fori_loop(0, frames, convolve, 0)

    for step in range(4, steps + 1):
        z_arrive(step)
    for step in range(4, y_steps + 1):
        for part in (0, 1):
            a_arrive(step, part)
    activated = hidden[:, :, 0].reshape(nz * picks, 2 * units)
    grads = dot_tn(activated, rows[:, :, 1].reshape(nz * picks, width))
    gout_ref[...] = grads[:units]
    grads_to[0] = grads[units:]
    g_copies = [remote(grads_to.at[0], grads_from.at[0], g_send.at[0], g_recv.at[0],
                       (x, partner, y))]
    grad_pre = hidden[:, :, 1].reshape(nz * picks, 2 * units)
    grads = dot_tn(grad_pre, rows[:, :, 0].reshape(nz * picks, width))
    grads_own[...] = grads[:units]
    grads_to[1] = grads[units:]
    g_copies.append(remote(grads_to.at[1], grads_from.at[1], g_send.at[1], g_recv.at[1],
                           (x, partner, y)))
    g_copies[0].wait_recv()
    gout_ref[...] += grads_from[0]
    g_copies[1].wait_recv()
    gin_ref[...] = jnp.transpose(grads_own[...] + grads_from[1])

    for copy in pending:
        copy.wait_send()


def on_device(
    nx, nh, ny,
    saved_conv, grad_out, conv_kernel, weight_in, weight_out, gate_values, picked_slots, slot_counts,
):
    nz = nh // 2
    frames, grid_rows, columns, width = saved_conv.shape
    tokens = frames * grid_rows * columns
    experts, _, units = weight_in.shape
    slot = picked_slots.shape[3]
    picks = experts * slot
    vmem = pl.BlockSpec(memory_space=pltpu.VMEM)
    hbm = pl.BlockSpec(memory_space=pltpu.HBM)
    steps = nz // 2
    dma = pltpu.SemaphoreType.DMA
    out, grad_in, grad_w = pl.pallas_call(
        functools.partial(body, nx, nh, ny),
        out_shape=(
            jax.ShapeDtypeStruct((frames, grid_rows, columns, width), FULL),
            jax.ShapeDtypeStruct((width, units), FULL),
            jax.ShapeDtypeStruct((units, width), FULL),
        ),
        in_specs=[hbm] * 8,
        out_specs=(vmem, vmem, vmem),
        scratch_shapes=[
            pltpu.VMEM((tokens, width), HALF),
            pltpu.VMEM((tokens, width), HALF),
            pltpu.VMEM(conv_kernel.shape, FULL),
            pltpu.VMEM(gate_values.shape[1:], FULL),
            pltpu.VMEM((experts, slot), jnp.int32),
            pltpu.VMEM((1, experts), jnp.int32),
            pltpu.VMEM((experts, 2, slot, width), HALF),
            pltpu.VMEM((nz, nx, 2, slot, width), HALF),
            pltpu.VMEM((nz, width, 2 * units), HALF),
            pltpu.VMEM((nz, 2 * units, width), HALF),
            pltpu.VMEM((ny, nz, 2, slot, 2 * units), HALF),
            pltpu.VMEM((ny, nz, 2, slot, 2 * units), HALF),
            pltpu.VMEM((2, nz, 2, slot, 2 * units), HALF),
            pltpu.VMEM((nz, ny, 2, slot, 2 * units), HALF),
            pltpu.VMEM((nz, 2, slot, 2 * units), HALF),
            pltpu.VMEM((nz, ny, slot, 2 * units), HALF),
            pltpu.VMEM((nx, slot, width), HALF),
            pltpu.VMEM((nx, slot, width), HALF),
            pltpu.VMEM((units, width), FULL),
            pltpu.VMEM((2, units, width), FULL),
            pltpu.VMEM((2, units, width), FULL),
            pltpu.VMEM((frames, grid_rows, columns, width), FULL),
            pltpu.VMEM((frames + 2, grid_rows + 2, columns, width), HALF),
            pltpu.VMEM((3, frames + 2, grid_rows + 2, columns, width), FULL),
            dma((6,)), dma((nx,)), dma((nx,)),
            dma((2,)), dma((2,)), dma((2,)),
            dma((4 * steps,)), dma((4 * steps,)), dma((4 * steps,)), dma((4 * steps,)),
            dma((8 * steps,)), dma((8 * steps,)),
            dma(((steps + 1) * ny,)), dma(((steps + 1) * ny,)),
            dma((nz,)), dma((nz,)),
            dma(((steps + 1) * ny,)), dma(((steps + 1) * ny,)),
            dma((2 * ny,)), dma((2 * ny,)),
            dma((nx,)), dma((nx,)),
            dma((2,)), dma((2,)),
            dma((8,)), dma((8,)),
        ],
        compiler_params=pltpu.CompilerParams(
            collective_id=0, has_side_effects=True, vmem_limit_bytes=62 * 1024 * 1024
        ),
    )(
        saved_conv.reshape(tokens, width),
        grad_out.reshape(tokens, width),
        conv_kernel,
        weight_in,
        weight_out,
        gate_values.reshape(gate_values.shape[1:]),
        picked_slots.reshape(experts, slot),
        slot_counts.reshape(1, experts),
    )
    return out, grad_in[None], grad_w[None]


def solution(mesh):
    placed = (
        P("tm", "height", None, "expert"),
        P("tm", "height", None, "expert"),
        P(None, "expert"),
        P(None, "expert", "height"),
        P(None, "height", "expert"),
        P("tm", None, None),
        P("tm", "height", None, None),
        P("tm", "height", None),
    )
    sizes = (mesh.shape["tm"], mesh.shape["height"], mesh.shape["expert"])
    return jax.shard_map(
        functools.partial(on_device, *sizes),
        mesh=mesh,
        in_specs=placed,
        out_specs=(
            P("tm", "height", None, "expert"),
            P("tm", "expert", "height"),
            P("tm", "height", "expert"),
        ),
        check_vma=False,
    )
```

time: 116 us -> 97.3 us (0.84)
  Pallas kernels: 106 us -> 92.7 us
  local copies, waits for them, and re-layouts: 8.76 us -> 3.67 us
    pallas_call x1, Pallas kernels: 106 us -> 92.7 us  [on_device(): pl.pallas_call(functools.partial(body, nx, nh, ny), out_shape=(jax.ShapeD...]
    unnamed x19 -> x7, local copies, waits for them, and re-layouts: 8.76 us -> 3.67 us
where the time goes in v2:
time: 97.3 us; the launch traced here: 97 us
  Pallas kernels  92.7 us (95%)
  local copies, waits for them, and re-layouts  3.67 us (4%)
    pallas_call x1, Pallas kernels, on_device(): pl.pallas_call(functools.partial(body, nx, nh, ny), out_shape=(jax.ShapeD...  92.7 us
    unnamed x7, local copies, waits for them, and re-layouts  3.67 us

profile of v2, /device:TPU:1, one launch (start us, length us, event | category | flops | bytes accessed | tf_op | source)
XLA Modules:
  0.0 97.0 jit_solution(13563569092372013171)
XLA Ops:
  0.6 92.7 %shard_map.103 = (f32[4,4,16,512]{3,2,1,0:T(8,128)}, f32[512,128]{1,0:T(8,128)}, f32[128,512]{1,0:T(8,128)}) custom-call(bf16[256,512]{1,0:T(8,128)(2,1)} %bitcast.7, bf16[256,512]{1,0:T(8,128)(2,1)} %bitcast.8, f32[27,512]{1,0:T(8,128)} %taps_hbm.1, bf16[8,512,128]{2,1,0:T(8,128)(2,1)} %win_ref.1, bf16[8,128,512]{2,1,0:T(8,128)(2,1)} %wout_ref.1, ...), custom_call_target="tpu_custom_call" | custom-call | tf_op jit(solution)/shard_map/pallas_call | solution.py:552
  93.4 0.0 copy-start.1
  93.4 1.9 %copy.14 = f32[4,4,16,512]{3,2,1,0:T(8,128)} copy(f32[4,4,16,512]{3,2,1,0:T(8,128)} %get-tuple-element.12) | data formatting | bytes 1048576
  95.3 0.0 copy-done.1
  95.3 0.0 copy-start
  95.3 0.7 copy.15
  96.0 0.3 copy-done
  96.3 0.7 copy.16
Async XLA Ops:
  93.4 1.9 %copy-start.1 = (f32[512,128]{1,0:T(8,128)S(1)}, f32[512,128]{1,0:T(8,128)}, u32[]{:S(2)}) copy-start(f32[512,128]{1,0:T(8,128)} %get-tuple-element.7) | copy-start | bytes 786436
  95.3 1.0 %copy-start = (f32[128,512]{1,0:T(8,128)S(1)}, f32[128,512]{1,0:T(8,128)}, u32[]{:S(2)}) copy-start(f32[128,512]{1,0:T(8,128)} %get-tuple-element.8) | copy-start | bytes 786436

commit v3 on v2

--- a/solution.py
+++ b/solution.py
@@ -120,6 +120,54 @@
     ]
     for copy in inputs + own_weights:
         copy.start()
+
+    pl.semaphore_wait(barrier, len(peers))
+
+    weight_copies = [
+        remote(win_ref.at[x], w_in.at[0, :, other], w_send.at[0], w_recv.at[0],
+               (x, partner, y)),
+        remote(wout_ref.at[x], w_out.at[0, other], w_send.at[1], w_recv.at[1],
+               (x, partner, y)),
+    ]
+
+    v_copies, u_copies = {}, {}
+
+    def v_block(step, way):
+        return z_at[(step if way else nz - step) % nz]
+
+    def v_half(block, part, half):
+        return w_out.at[block, half] if part else w_in.at[block, :, half]
+
+    def v_goes(step, part, way):
+        return step < steps or (step == steps and part == way)
+
+    def v_forward(step, part, way):
+        key = ((step - 1) * 2 + part) * 2 + way
+        if step == 1:
+            source = (wout_ref if part else win_ref).at[x]
+        else:
+            source = v_half(v_block(step - 1, way), part, own)
+        v_copies[step, part, way] = remote(
+            source, v_half(v_block(step, way), part, own), v_send.at[key], v_recv.at[key],
+            onward(way),
+        )
+
+    def v_arrive(step):
+        for part in (0, 1):
+            for way in (0, 1):
+                if v_goes(step, part, way):
+                    v_copies[step, part, way].wait_recv()
+                    if step < steps and v_goes(step + 1, part, way):
+                        v_forward(step + 1, part, way)
+                    block, key = v_block(step, way), ((step - 1) * 2 + part) * 2 + way
+                    u_copies[step, part, way] = remote(
+                        v_half(block, part, own), v_half(block, part, other),
+                        u_send.at[key], u_recv.at[key], (x, partner, y),
+                    )
+
+    for way in (0, 1):
+        if v_goes(1, 0, way):
+            v_forward(1, 0, way)
 
     lane = lax.broadcasted_iota(jnp.int32, (nx, picks), 1)
     expert_row = lax.broadcasted_iota(jnp.int32, (nx, picks), 0)
@@ -158,8 +206,6 @@
     chosen[:, 1] = grad_rows.reshape(nx, slot, width)
     rows[0, 0] = chosen[x]
 
-    pl.semaphore_wait(barrier, len(peers))
-
     x_copies = {}
     for d in x_order[1:]:
         there = x_at[nx - d]
@@ -167,48 +213,6 @@
             chosen.at[x_far(d)], rows.at[0, there], x_send.at[there], x_recv.at[there],
             (x_far(d), h, y),
         )
-    weight_copies = [
-        remote(win_ref.at[x], w_in.at[0, :, other], w_send.at[0], w_recv.at[0],
-               (x, partner, y)),
-        remote(wout_ref.at[x], w_out.at[0, other], w_send.at[1], w_recv.at[1],
-               (x, partner, y)),
-    ]
-
-    v_copies, u_copies = {}, {}
-
-    def v_block(step, way):
-        return z_at[(step if way else nz - step) % nz]
-
-    def v_half(block, part, half):
-        return w_out.at[block, half] if part else w_in.at[block, :, half]
-
-    def v_goes(step, part, way):
-        return step < steps or (step == steps and part == way)
-
-    def v_forward(step, part, way):
-        key = ((step - 1) * 2 + part) * 2 + way
-        if step == 1:
-            source = (wout_ref if part else win_ref).at[x]
-        else:
-            source = v_half(v_block(step - 1, way), part, own)
-        v_copies[step, part, way] = remote(
-            source, v_half(v_block(step, way), part, own), v_send.at[key], v_recv.at[key],
-            onward(way),
-        )
-
-    def v_arrive(step):
-        for part in (0, 1):
-            for way in (0, 1):
-                if v_goes(step, part, way):
-                    v_copies[step, part, way].wait_recv()
-                    if step < steps and v_goes(step + 1, part, way):
-                        v_forward(step + 1, part, way)
-                    block, key = v_block(step, way), ((step - 1) * 2 + part) * 2 + way
-                    u_copies[step, part, way] = remote(
-                        v_half(block, part, own), v_half(block, part, other),
-                        u_send.at[key], u_recv.at[key], (x, partner, y),
-                    )
-
     parts = min(2, nx)
     split = nx // parts
     z_copies = {}
@@ -226,11 +230,10 @@
     def z_goes(step, part, way):
         return step < steps or (step == steps and (2 * part // parts) == way)
 
-    def z_start():
-        for part in range(parts):
-            for way in (0, 1):
-                if z_goes(1, part, way):
-                    z_forward(1, part, way)
+    def z_start(part):
+        for way in (0, 1):
+            if z_goes(1, part, way):
+                z_forward(1, part, way)
 
     def z_arrive(step):
         if step > steps:
@@ -351,28 +354,29 @@
             e_send_to(stage, 4 + way, pre_grads.at[span, source], way)
             e_send_to(stage, 4 if way == 1 else 0, pre_grads.at[lines, source], 2 * way)
 
-    for part in (0, 1):
-        for way in (0, 1):
-            if v_goes(1, part, way):
-                v_forward(1, part, way)
-    v_arrive(1)
-    for copy in x_copies.values():
-        copy.wait_recv()
     for copy in own_weights:
         copy.wait()
     for copy in weight_copies:
+        copy.wait_recv()
+    for way in (0, 1):
+        if v_goes(1, 1, way):
+            v_forward(1, 1, way)
+    v_arrive(1)
+    for copy in x_copies.values():
         copy.wait_recv()
     partial_sums(0)
     for stage in range(1, last_stage + 1):
         v_arrive(stage + 1)
         if stage == max(last_stage - 1, 1):
-            z_start()
+            for part in range(parts):
+                z_start(part)
         partial_sums(stage)
         relay_sums(stage - 1)
         if stage >= 2:
             own_hidden(stage - 2)
     if last_stage >= 1:
         own_hidden(last_stage - 1)
+    z_arrive(1)
 
     y_steps = ny // 2
     bound = spans[max(last_stage - 2, 0)][1]
@@ -407,11 +411,10 @@
                 if step < y_steps and a_goes(step + 1, part, way):
                     a_forward(step + 1, part, way)
 
-    for stage in range(last_stage - 1):
+    for stage in range(last_stage):
         relay_grads(stage)
-    z_arrive(1)
+    own_hidden(last_stage)
     a_start(0)
-    own_hidden(last_stage)
     z_arrive(2)
     a_start(1)
     a_arrive(1, 0)

time: 97.3 us -> 94.7 us (0.973)
  Pallas kernels: 92.7 us -> 90.2 us
    pallas_call x1, Pallas kernels: 92.7 us -> 90.2 us  [on_device(): pl.pallas_call(functools.partial(body, nx, nh, ny), out_shape=(jax.ShapeD...]
where the time goes in v3:
time: 94.7 us; the launch traced here: 94.5 us
  Pallas kernels  90.2 us (95%)
  local copies, waits for them, and re-layouts  3.67 us (4%)
    pallas_call x1, Pallas kernels, on_device(): pl.pallas_call(functools.partial(body, nx, nh, ny), out_shape=(jax.ShapeD...  90.2 us
    unnamed x7, local copies, waits for them, and re-layouts  3.67 us

profile of v3, /device:TPU:1, one launch (start us, length us, event | category | flops | bytes accessed | tf_op | source)
XLA Modules:
  0.0 94.5 jit_solution(7891843658140562995)
XLA Ops:
  0.6 90.2 %shard_map.103 = (f32[4,4,16,512]{3,2,1,0:T(8,128)}, f32[512,128]{1,0:T(8,128)}, f32[128,512]{1,0:T(8,128)}) custom-call(bf16[256,512]{1,0:T(8,128)(2,1)} %bitcast.7, bf16[256,512]{1,0:T(8,128)(2,1)} %bitcast.8, f32[27,512]{1,0:T(8,128)} %taps_hbm.1, bf16[8,512,128]{2,1,0:T(8,128)(2,1)} %win_ref.1, bf16[8,128,512]{2,1,0:T(8,128)(2,1)} %wout_ref.1, ...), custom_call_target="tpu_custom_call" | custom-call | tf_op jit(solution)/shard_map/pallas_call | solution.py:555
  90.8 0.0 copy-start.1
  90.8 1.9 %copy.14 = f32[4,4,16,512]{3,2,1,0:T(8,128)} copy(f32[4,4,16,512]{3,2,1,0:T(8,128)} %get-tuple-element.12) | data formatting | bytes 1048576
  92.8 0.0 copy-done.1
  92.8 0.0 copy-start
  92.8 0.7 copy.15
  93.5 0.3 copy-done
  93.8 0.7 copy.16
Async XLA Ops:
  90.8 1.9 %copy-start.1 = (f32[512,128]{1,0:T(8,128)S(1)}, f32[512,128]{1,0:T(8,128)}, u32[]{:S(2)}) copy-start(f32[512,128]{1,0:T(8,128)} %get-tuple-element.7) | copy-start | bytes 786436
  92.8 1.0 %copy-start = (f32[128,512]{1,0:T(8,128)S(1)}, f32[128,512]{1,0:T(8,128)}, u32[]{:S(2)}) copy-start(f32[128,512]{1,0:T(8,128)} %get-tuple-element.8) | copy-start | bytes 786436
